TPU v7x, 256 devices: a whole 4x4x8 slice. The times are simulated.
256 devices in a mesh: row: 16 (over x, z_hi), col: 16 (over y, z_lo, core).
Axes of the slice: x: 4, y: 4, z: 8 (z_hi: 4, z_lo: 2; z = z_hi * 2 + z_lo), core: 2. Of those that a mesh axis runs over, the one named last changes fastest.
Arguments:
- left_panels: bfloat16 [8192, 16384], P('row', 'col'), may hold values from -0.09375 to 0.09375
- right_panels: bfloat16 [16384, 32768], P('row', 'col'), may hold values from -6 to 6
- left_pattern: int32 [64, 128], P('row', 'col'), may hold values from 0 to 1, as said below
- right_pattern: int32 [128, 256], P('row', 'col'), may hold values from 0 to 1, as said below
Outputs:
- square_part: bfloat16 [8192, 32768], P('row', 'col')
Inputs may be any that keep to these rules, and one draw needn't show every extreme that they name: `left_pattern`: entries are 0 or 1. In every block of 4 x 8 tiles held by one device at most 24 tiles are 1, and exactly 24 in at least one block. `right_pattern`: entries are 0 or 1. In every block of 8 x 16 tiles held by one device at most 96 tiles are 1, and exactly 96 in at least one block.
All inputs are finite; a program needn't handle non-finite values.
Results may differ from a plain program's by a relative error of at most 0.001.
Values may be sent and summed in bfloat16 or wider, within the bound.
A program may use at most 128 MiB of HBM per device.

v0:
```python
import jax
import jax.numpy as jnp
from jax import lax
from jax.sharding import PartitionSpec as P

TILE = 128
STEPS = 4


def shifted(value, axis, steps):
    count = lax.axis_size(axis)
    pairs = [(source, (source + steps) % count) for source in range(count)]
    return lax.ppermute(value, axis, pairs)


def mask_tiles(matrix, occupancy):
    tile_rows, tile_cols = occupancy.shape
    view = matrix.reshape(tile_rows, TILE, tile_cols, TILE)
    view = view * occupancy.astype(matrix.dtype)[:, None, :, None]
    return view.reshape(matrix.shape)


def per_device(left_panels, right_panels, left_pattern, right_pattern):
    masked_left = mask_tiles(left_panels, left_pattern)
    masked_right = mask_tiles(right_panels, right_pattern)
    running = jnp.dot(masked_left, masked_right, preferred_element_type=jnp.float32)
    for offset in range(1, STEPS):
        masked_left = shifted(masked_left, "col", -1)
        masked_right = shifted(masked_right, "row", -1)
        running = running + jnp.dot(masked_left, masked_right, preferred_element_type=jnp.float32)
    return running.astype(jnp.bfloat16)


def solution(mesh):
    placed = (P("row", "col"), P("row", "col"), P("row", "col"), P("row", "col"))
    return jax.shard_map(
        per_device, mesh=mesh, in_specs=placed, out_specs=P("row", "col"), check_vma=False
    )
```

profile of v0, /device:TPU:1, one launch (start us, length us, event | category | flops | bytes accessed | tf_op | source)
XLA Modules:
  0.0 605.2 jit_solution(9814589266693880712)
XLA Ops:
  0.0 0.0 copy-start
  0.0 0.8 convert_element_type.10
  0.8 0.6 mul.25
  1.5 0.7 copy-done
  2.2 0.0 copy-start.2
  2.2 0.0 copy-start.1
  2.2 0.9 bitcast_multiply_fusion
  3.1 9.1 %collective-permute-start.1 = (bf16[1024,2048]{1,0:T(8,128)(2,1)S(1)}, bf16[1024,2048]{1,0:T(8,128)(2,1)S(1)}, u32[]{:S(2)}, u32[]{:S(2)}) collective-permute-start(bf16[1024,2048]{1,0:T(8,128)(2,1)S(1)} %bitcast_multiply_fusion), channel_id=1, source_target_pairs={{0,240},{16,0},{32,16},{48,32},{64,48},{80,64},{96,80},{112,96},{1... | collective-permute-start | bytes 12582920 | tf_op jit(solution)/shard_map/ppermute | solution.py:13
  12.2 179.4 %collective-permute-done.1 = bf16[1024,2048]{1,0:T(8,128)(2,1)S(1)} collective-permute-done((bf16[1024,2048]{1,0:T(8,128)(2,1)S(1)}, bf16[1024,2048]{1,0:T(8,128)(2,1)S(1)}, u32[]{:S(2)}, u32[]{:S(2)}) %collective-permute-start.1) | collective-permute-done | bytes 4194336 | tf_op jit(solution)/shard_map/ppermute | solution.py:13
  191.7 6.6 %collective-permute-start.3 = (bf16[1024,2048]{1,0:T(8,128)(2,1)S(1)}, bf16[1024,2048]{1,0:T(8,128)(2,1)S(1)}, u32[]{:S(2)}, u32[]{:S(2)}) collective-permute-start(bf16[1024,2048]{1,0:T(8,128)(2,1)S(1)} %collective-permute-done.1), channel_id=1, source_target_pairs={{0,240},{16,0},{32,16},{48,32},{64,48},{80,64},{96,80},{112,96},{1... | collective-permute-start | bytes 12582920 | tf_op jit(solution)/shard_map/ppermute | solution.py:13
  198.2 178.9 %collective-permute-done.3 = bf16[1024,2048]{1,0:T(8,128)(2,1)S(1)} collective-permute-done((bf16[1024,2048]{1,0:T(8,128)(2,1)S(1)}, bf16[1024,2048]{1,0:T(8,128)(2,1)S(1)}, u32[]{:S(2)}, u32[]{:S(2)}) %collective-permute-start.3) | collective-permute-done | bytes 4194336 | tf_op jit(solution)/shard_map/ppermute | solution.py:13
  377.1 6.6 %collective-permute-start.5 = (bf16[1024,2048]{1,0:T(8,128)(2,1)S(1)}, bf16[1024,2048]{1,0:T(8,128)(2,1)S(1)}, u32[]{:S(2)}, u32[]{:S(2)}) collective-permute-start(bf16[1024,2048]{1,0:T(8,128)(2,1)S(1)} %collective-permute-done.3), channel_id=1, source_target_pairs={{0,240},{16,0},{32,16},{48,32},{64,48},{80,64},{96,80},{112,96},{1... | collective-permute-start | bytes 12582920 | tf_op jit(solution)/shard_map/ppermute | solution.py:13
  383.7 0.0 copy-done.2
  383.7 0.2 mul.22
  383.9 0.0 copy-done.1
  383.9 0.1 bitcast_multiply_fusion.1
  384.0 1.0 collective-permute-start
  385.0 187.9 %collective-permute-done = bf16[512,1024]{1,0:T(8,128)(2,1)S(1)} collective-permute-done((bf16[512,1024]{1,0:T(8,128)(2,1)S(1)}, bf16[512,1024]{1,0:T(8,128)(2,1)S(1)}, u32[]{:S(2)}, u32[]{:S(2)}) %collective-permute-start) | collective-permute-done | bytes 1048608 | tf_op jit(solution)/shard_map/ppermute | solution.py:13
  572.9 0.0 collective-permute-start.2
  572.9 2.4 fusion
  575.3 11.8 %collective-permute-done.2 = bf16[512,1024]{1,0:T(8,128)(2,1)S(1)} collective-permute-done((bf16[512,1024]{1,0:T(8,128)(2,1)S(1)}, bf16[512,1024]{1,0:T(8,128)(2,1)S(1)}, u32[]{:S(2)}, u32[]{:S(2)}) %collective-permute-start.2) | collective-permute-done | bytes 1048608 | tf_op jit(solution)/shard_map/ppermute | solution.py:13
  587.1 0.0 collective-permute-start.4
  587.1 2.4 fusion.1
  589.5 2.4 fusion.2
  591.8 9.5 %collective-permute-done.4 = bf16[512,1024]{1,0:T(8,128)(2,1)S(1)} collective-permute-done((bf16[512,1024]{1,0:T(8,128)(2,1)S(1)}, bf16[512,1024]{1,0:T(8,128)(2,1)S(1)}, u32[]{:S(2)}, u32[]{:S(2)}) %collective-permute-start.4) | collective-permute-done | bytes 1048608 | tf_op jit(solution)/shard_map/ppermute | solution.py:13
  601.3 0.0 collective-permute-done.5
  601.3 3.8 add_convert_fusion
  (1 shorter events, 0.0 us)
Async XLA Ops:
  0.0 2.2 copy-start
  2.2 381.5 %copy-start.2 = (s32[4,8]{1,0:T(4,128)S(1)}, s32[4,8]{1,0:T(4,128)}, u32[]{:S(2)}) copy-start(s32[4,8]{1,0:T(4,128)} %param.6) | copy-start | bytes 388
  2.2 381.7 %copy-start.1 = (bf16[512,1024]{1,0:T(8,128)(2,1)S(1)}, bf16[512,1024]{1,0:T(8,128)(2,1)}, u32[]{:S(2)}) copy-start(bf16[512,1024]{1,0:T(8,128)(2,1)} %param.4) | copy-start | bytes 3145732
  3.1 188.6 %collective-permute-start.1 = (bf16[1024,2048]{1,0:T(8,128)(2,1)S(1)}, bf16[1024,2048]{1,0:T(8,128)(2,1)S(1)}, u32[]{:S(2)}, u32[]{:S(2)}) collective-permute-start(bf16[1024,2048]{1,0:T(8,128)(2,1)S(1)} %bitcast_multiply_fusion), channel_id=1, source_target_pairs={{0,240},{16,0},{32,16},{48,32},{64,48},{80,64},{96,80},{112,96},{1... | collective-permute-start | bytes 12582920 | tf_op jit(solution)/shard_map/ppermute | solution.py:13
  191.7 185.4 %collective-permute-start.3 = (bf16[1024,2048]{1,0:T(8,128)(2,1)S(1)}, bf16[1024,2048]{1,0:T(8,128)(2,1)S(1)}, u32[]{:S(2)}, u32[]{:S(2)}) collective-permute-start(bf16[1024,2048]{1,0:T(8,128)(2,1)S(1)} %collective-permute-done.1), channel_id=1, source_target_pairs={{0,240},{16,0},{32,16},{48,32},{64,48},{80,64},{96,80},{112,96},{1... | collective-permute-start | bytes 12582920 | tf_op jit(solution)/shard_map/ppermute | solution.py:13
  377.1 224.2 %collective-permute-start.5 = (bf16[1024,2048]{1,0:T(8,128)(2,1)S(1)}, bf16[1024,2048]{1,0:T(8,128)(2,1)S(1)}, u32[]{:S(2)}, u32[]{:S(2)}) collective-permute-start(bf16[1024,2048]{1,0:T(8,128)(2,1)S(1)} %collective-permute-done.3), channel_id=1, source_target_pairs={{0,240},{16,0},{32,16},{48,32},{64,48},{80,64},{96,80},{112,96},{1... | collective-permute-start | bytes 12582920 | tf_op jit(solution)/shard_map/ppermute | solution.py:13
  384.0 188.8 %collective-permute-start = (bf16[512,1024]{1,0:T(8,128)(2,1)S(1)}, bf16[512,1024]{1,0:T(8,128)(2,1)S(1)}, u32[]{:S(2)}, u32[]{:S(2)}) collective-permute-start(bf16[512,1024]{1,0:T(8,128)(2,1)S(1)} %bitcast_multiply_fusion.1), channel_id=1, source_target_pairs={{0,15},{1,0},{2,1},{3,2},{4,3},{5,4},{6,5},{7,6},{8,7},{9,8},{10,9... | collective-permute-start | bytes 3145736 | tf_op jit(solution)/shard_map/ppermute | solution.py:13
  572.9 14.2 %collective-permute-start.2 = (bf16[512,1024]{1,0:T(8,128)(2,1)S(1)}, bf16[512,1024]{1,0:T(8,128)(2,1)S(1)}, u32[]{:S(2)}, u32[]{:S(2)}) collective-permute-start(bf16[512,1024]{1,0:T(8,128)(2,1)S(1)} %collective-permute-done), channel_id=1, source_target_pairs={{0,15},{1,0},{2,1},{3,2},{4,3},{5,4},{6,5},{7,6},{8,7},{9,8},{10,9... | collective-permute-start | bytes 3145736 | tf_op jit(solution)/shard_map/ppermute | solution.py:13
  587.1 14.2 %collective-permute-start.4 = (bf16[512,1024]{1,0:T(8,128)(2,1)S(1)}, bf16[512,1024]{1,0:T(8,128)(2,1)S(1)}, u32[]{:S(2)}, u32[]{:S(2)}) collective-permute-start(bf16[512,1024]{1,0:T(8,128)(2,1)S(1)} %collective-permute-done.2), channel_id=1, source_target_pairs={{0,15},{1,0},{2,1},{3,2},{4,3},{5,4},{6,5},{7,6},{8,7},{9,8},{10,9... | collective-permute-start | bytes 3145736 | tf_op jit(solution)/shard_map/ppermute | solution.py:13
where the time goes:
time: 605 us
  waiting for transfers between devices  568 us (94%)
  starting transfers between devices  23.2 us (4%)
  matrix products  10.9 us (2%)
    ppermute x6, waiting for transfers between devices, shifted(): return lax.ppermute(value, axis, pairs)  568 us
    ppermute x6, starting transfers between devices, shifted(): return lax.ppermute(value, axis, pairs)  23.2 us
  transfers between devices with their start and end apart: 6, of which 5 were waited for; matrix products, arithmetic and copies ran while one was open for 1% of the time, Pallas kernels for 0%

commit v1 on v0

v1 whole, which is shorter than its diff:
```python
import functools

import jax
import jax.numpy as jnp
from jax import lax
from jax.experimental import pallas as pl
from jax.experimental.pallas import tpu as pltpu
from jax.sharding import PartitionSpec as P

TILE = 128
RT, KT, CT = 4, 8, 16
CAP, CAPB = 24, 96
CHUNKS = 4
PER = CAPB // CHUNKS
WIDE = 256
PIECES = CT * TILE // WIDE
GROUPS = 8
SPAN = RT * TILE // GROUPS
TOP = 32767.0
MESH = pl.DeviceIdType.MESH
SLOT_B, SLOT_A, PICK_B, PICK_A = 0, 1, 2, 3
LOCAL, WITH_OWN, WITH_NEXT, NEXT, FAR = range(5)


def tables_kernel(left_ref, right_ref, table_ref):
    def clear(i, carry):
        table_ref[PICK_B, i] = 0
        table_ref[PICK_A, i] = 0
        table_ref[SLOT_A, i] = CAP
        return carry

    lax.fori_loop(0, TILE, clear, 0)

    def walk_right(t, taken):
        there = right_ref[t % KT, t // KT]
        table_ref[PICK_B, jnp.minimum(taken, TILE - 1)] = t
        table_ref[SLOT_B, t] = jnp.where(there > 0, taken, CAPB)
        return taken + jnp.where(there > 0, 1, 0)

    lax.fori_loop(0, KT * CT, walk_right, 0)

    def walk_left(t, taken):
        there = left_ref[t % RT, t // RT]
        table_ref[PICK_A, jnp.minimum(taken, TILE - 1)] = t
        table_ref[SLOT_A, t] = jnp.where(there > 0, taken, CAP)
        return taken + jnp.where(there > 0, 1, 0)

    lax.fori_loop(0, RT * KT, walk_left, 0)


def main_kernel(
    a_ref, b_ref, table_ref, table_hbm, out_ref,
    a_in, b_in, a_pack, b_pack, a_got, b_got, b_stage, table_got, table_at,
    a_full, b_full, total, part, code_out, scale_out, code_in, scale_in, result,
    local_sem, table_send, table_recv, a_send, a_recv, b_send, b_recv, p_send, p_recv, out_sem,
):
    n_row, n_col = lax.axis_size("row"), lax.axis_size("col")
    row, col = lax.axis_index("row"), lax.axis_index("col")
    odd = lax.rem(row + col, 2)

    def at(i, j):
        return (lax.rem(row + i + n_row, n_row), lax.rem(col + j + n_col, n_col))

    targets = (at(0, 2 * odd - 3), at(1 + 2 * odd, -1 - 2 * odd), at(3 - 2 * odd, -2), at(1 - 2 * odd, 0), at(-4, 0))
    sources = (at(0, 1 + 2 * odd), at(-1 - 2 * odd, 1 + 2 * odd), at(-1 - 2 * odd, 2), at(1 - 2 * odd, 0), at(4, 0))
    p_target, p_source = at(-1 - 2 * odd, 0), at(3 - 2 * odd, 0)

    barrier = pltpu.get_barrier_semaphore()
    for source in (*sources[:4], p_source):
        pl.semaphore_signal(barrier, inc=1, device_id=source, device_id_type=MESH)

    @pl.when(odd == 1)
    def _():
        pl.semaphore_signal(barrier, inc=1, device_id=sources[FAR], device_id_type=MESH)

    def load_a(k):
        return pltpu.make_async_copy(
            a_ref.at[:, :, pl.ds(k * TILE, TILE)], a_in.at[pl.ds(k * RT, RT)], local_sem.at[k])

    def load_b(c):
        return pltpu.make_async_copy(
            b_ref.at[:, :, pl.ds(c * TILE, TILE)], b_in.at[pl.ds(c * KT, KT)], local_sem.at[KT + c])

    for k in range(KT):
        load_a(k).start()
    for c in range(CT):
        load_b(c).start()

    blank = jnp.zeros((TILE, TILE), jnp.bfloat16)
    a_pack[CAP] = blank
    b_pack[CAPB] = blank
    for i in range(3):
        a_got[i, CAP] = blank
    b_got[1, CAPB] = blank
    b_stage[CAPB] = blank

    def pack_a(n, carry):
        a_pack[n] = a_in[table_ref[PICK_A, n]]
        return carry

    def pack_b(n, carry):
        b_pack[n] = b_in[table_ref[PICK_B, n]]
        return carry

    def stage_b(n, carry):
        b_stage[n] = b_got[0, n]
        return carry

    def send_table(i, source):
        return pltpu.make_async_remote_copy(
            source, table_got.at[i], table_send.at[i], table_recv.at[i], device_id=targets[i], device_id_type=MESH)

    def send_a(i):
        return pltpu.make_async_remote_copy(
            a_pack.at[pl.ds(0, CAP)], a_got.at[i, pl.ds(0, CAP)], a_send.at[i], a_recv.at[i],
            device_id=targets[i], device_id_type=MESH)

    def send_b(i, q, source):
        where = pl.ds(q * PER, PER)
        return pltpu.make_async_remote_copy(
            source.at[where], b_got.at[i, where], b_send.at[i, q], b_recv.at[i, q],
            device_id=targets[NEXT + i], device_id_type=MESH)

    def send_code(c):
        return pltpu.make_async_remote_copy(
            code_out.at[c], code_in.at[c], p_send.at[0, c], p_recv.at[0, c], device_id=p_target, device_id_type=MESH)

    def send_scale(c):
        return pltpu.make_async_remote_copy(
            scale_out.at[c], scale_in.at[c], p_send.at[1, c], p_recv.at[1, c], device_id=p_target, device_id_type=MESH)

    for k in range(KT):
        load_a(k).wait()
    lax.fori_loop(0, CAP, pack_a, 0)
    pl.semaphore_wait(barrier, 5 + odd)
    for i in range(4):
        send_table(i, table_hbm).start()
    for i in (WITH_OWN, WITH_NEXT, LOCAL):
        send_a(i).start()
    for c in range(CT):
        load_b(c).wait()
    for q in range(CHUNKS):
        lax.fori_loop(q * PER, (q + 1) * PER, pack_b, 0)
        send_b(0, q, b_pack).start()

    def unpack_a(i, tile_of):
        for k in range(KT):
            for r in range(RT):
                a_full[i, r * TILE : (r + 1) * TILE, k * TILE : (k + 1) * TILE] = tile_of(k * RT + r)

    def unpack_b(i, tile_of, first, last):
        def one(c, carry):
            for half in range(WIDE // TILE):
                for k in range(KT):
                    tile = tile_of((c * (WIDE // TILE) + half) * KT + k)
                    b_full[i, c, k * TILE : (k + 1) * TILE, half * TILE : (half + 1) * TILE] = tile
            return carry

        lax.fori_loop(first, last, one, 0)

    def product(i, j, c):
        return jnp.dot(a_full[i], b_full[j, c], preferred_element_type=jnp.float32)

    unpack_a(3, lambda t: a_pack[table_ref[SLOT_A, t]])
    unpack_b(0, lambda t: b_pack[table_ref[SLOT_B, t]], 0, PIECES)

    def first_term(c, carry):
        total[c] = product(3, 0, c)
        return carry

    lax.fori_loop(0, PIECES, first_term, 0)

    def fetch_table(i):
        send_table(i, table_hbm).wait_recv()
        fetch = pltpu.make_async_copy(table_got.at[i], table_at.at[i], local_sem.at[KT + CT])
        fetch.start()
        fetch.wait()

    for i in (WITH_OWN, WITH_NEXT, LOCAL):
        fetch_table(i)
        send_a(i).wait_recv()
    for i in (WITH_OWN, WITH_NEXT, LOCAL):
        unpack_a(i, lambda t: a_got[i, table_at[i, SLOT_A, t]])

    def part_own(c, carry):
        part[c] = product(WITH_OWN, 0, c)
        return carry

    lax.fori_loop(0, PIECES, part_own, 0)
    fetch_table(NEXT)

    @pl.when(odd == 1)
    def _():
        send_table(FAR, table_got.at[NEXT]).start()

    def send_part(c, carry):
        part[c] += product(WITH_NEXT, 1, c)
        for g in range(GROUPS):
            rows = slice(g * SPAN, (g + 1) * SPAN)
            values = part[c, rows, :]
            most = jnp.maximum(jnp.max(jnp.abs(values), axis=0, keepdims=True), 1e-33)
            code_out[c, rows, :] = jnp.round(values * (TOP / most)).astype(jnp.int32).astype(jnp.int16)
            scale_out[c, g : g + 1, :] = most * (1.0 / TOP)
        send_scale(c).start()
        send_code(c).start()
        return carry

    done = 0
    for q in range(CHUNKS):
        send_b(0, q, b_pack).wait_recv()

        @pl.when(odd == 1)
        def _():
            send_b(1, q, b_got.at[0]).start()

        lax.fori_loop(q * PER, (q + 1) * PER, stage_b, 0)
        ready = PIECES if q == CHUNKS - 1 else (q + 1) * PER // KT * TILE // WIDE
        if q >= CHUNKS - 2:
            unpack_b(1, lambda t: b_stage[table_at[NEXT, SLOT_B, t]], done, ready)
            lax.fori_loop(done, ready, send_part, 0)
            done = ready

    @pl.when(odd == 1)
    def _():
        fetch_table(FAR)
        for q in range(CHUNKS):
            send_b(1, q, b_got.at[0]).wait_recv()
        unpack_b(1, lambda t: b_got[1, table_at[FAR, SLOT_B, t]], 0, PIECES)

    def second_term(c, carry):
        total[c] += product(LOCAL, 1, c)
        return carry

    lax.fori_loop(0, PIECES, second_term, 0)

    def store(c):
        return pltpu.make_async_copy(result.at[c], out_ref.at[:, pl.ds(c * WIDE, WIDE)], out_sem.at[c])

    for c in range(PIECES):
        send_scale(c).wait_recv()
        send_code(c).wait_recv()
        for g in range(GROUPS):
            rows = slice(g * SPAN, (g + 1) * SPAN)
            other = code_in[c, rows, :].astype(jnp.int32).astype(jnp.float32) * scale_in[c, g : g + 1, :]
            result[c, rows, :] = (total[c, rows, :] + other).astype(jnp.bfloat16)
        store(c).start()

    for i in range(4):
        send_table(i, table_hbm).wait_send()
    for i in range(3):
        send_a(i).wait_send()
    for q in range(CHUNKS):
        send_b(0, q, b_pack).wait_send()

    @pl.when(odd == 1)
    def _():
        send_table(FAR, table_got.at[NEXT]).wait_send()
        for q in range(CHUNKS):
            send_b(1, q, b_got.at[0]).wait_send()

    for c in range(PIECES):
        send_scale(c).wait_send()
        send_code(c).wait_send()
        store(c).wait()


def per_device(left_panels, right_panels, left_pattern, right_pattern):
    smem = pl.BlockSpec(memory_space=pltpu.SMEM)
    anywhere = pl.BlockSpec(memory_space=pl.ANY)
    table = pl.pallas_call(
        tables_kernel,
        out_shape=jax.ShapeDtypeStruct((4, TILE), jnp.int32),
        in_specs=[smem, smem],
        out_specs=smem,
        name="tile_tables",
    )(left_pattern, right_pattern)
    rows, cols, inner = RT * TILE, CT * TILE, KT * TILE
    bf16, f32, dma = jnp.bfloat16, jnp.float32, pltpu.SemaphoreType.DMA
    return pl.pallas_call(
        main_kernel,
        out_shape=jax.ShapeDtypeStruct((rows, cols), bf16),
        in_specs=[anywhere, anywhere, smem, anywhere],
        out_specs=anywhere,
        scratch_shapes=[
            pltpu.VMEM((RT * KT, TILE, TILE), bf16),
            pltpu.VMEM((KT * CT, TILE, TILE), bf16),
            pltpu.VMEM((CAP + 1, TILE, TILE), bf16),
            pltpu.VMEM((CAPB + 1, TILE, TILE), bf16),
            pltpu.VMEM((3, CAP + 1, TILE, TILE), bf16),
            pltpu.VMEM((2, CAPB + 1, TILE, TILE), bf16),
            pltpu.VMEM((CAPB + 1, TILE, TILE), bf16),
            pltpu.VMEM((5, 4, TILE), jnp.int32),
            pltpu.SMEM((5, 4, TILE), jnp.int32),
            pltpu.VMEM((4, rows, inner), bf16),
            pltpu.VMEM((2, PIECES, inner, WIDE), bf16),
            pltpu.VMEM((PIECES, rows, WIDE), f32),
            pltpu.VMEM((PIECES, rows, WIDE), f32),
            pltpu.VMEM((PIECES, rows, WIDE), jnp.int16),
            pltpu.VMEM((PIECES, GROUPS, WIDE), f32),
            pltpu.VMEM((PIECES, rows, WIDE), jnp.int16),
            pltpu.VMEM((PIECES, GROUPS, WIDE), f32),
            pltpu.VMEM((PIECES, rows, WIDE), bf16),
            dma((KT + CT + 1,)),
            dma((5,)),
            dma((5,)),
            dma((3,)),
            dma((3,)),
            dma((2, CHUNKS)),
            dma((2, CHUNKS)),
            dma((2, PIECES)),
            dma((2, PIECES)),
            dma((PIECES,)),
        ],
        compiler_params=pltpu.CompilerParams(
            collective_id=0, has_side_effects=True, vmem_limit_bytes=60 * 2**20
        ),
        cost_estimate=pl.CostEstimate(flops=8 * rows * inner * cols, bytes_accessed=2**23, transcendentals=0),
        name="exchange_and_multiply",
    )(left_panels.reshape(RT, TILE, inner), right_panels.reshape(KT, TILE, cols), table, table)


def solution(mesh):
    placed = (P("row", "col"), P("row", "col"), P("row", "col"), P("row", "col"))
    return jax.shard_map(
        per_device, mesh=mesh, in_specs=placed, out_specs=P("row", "col"), check_vma=False
    )
```

time: 605 us -> 217 us (0.36)
  the two profiles are of different devices: /device:TPU:1 before, /device:TPU:201 now
where the time goes in v1:
time: 217 us
  Pallas kernels  214 us (99%)
  local copies, waits for them, and re-layouts  3.16 us (1%)
    pallas_call x1, Pallas kernels, per_device(): pl.pallas_call(main_kernel, out_shape=jax.ShapeDtypeStruct((rows, cols),...  209 us
    pallas_call x1, Pallas kernels, per_device(): pl.pallas_call(tables_kernel, out_shape=jax.ShapeDtypeStruct((4, TILE), j...  4.96 us

profile of v1, /device:TPU:201, one launch (start us, length us, event | category | flops | bytes accessed | tf_op | source)
XLA Modules:
  0.0 217.0 jit_solution(9898001073343831737)
XLA Ops:
  0.0 5.0 %tile_tables.1.table_ref.table_hbm = s32[4,128]{1,0:T(4,128)} custom-call(s32[4,8]{1,0:T(4,128)} %left_ref.1, s32[8,16]{1,0:T(8,128)} %right_ref.1), custom_call_target="tpu_custom_call" | custom-call | tf_op jit(solution)/shard_map/tile_tables/pallas_call | solution.py:270
  5.0 208.9 %exchange_and_multiply.1 = bf16[512,2048]{1,0:T(8,128)(2,1)} custom-call(bf16[4,128,1024]{2,1,0:T(8,128)(2,1)} %bitcast.3, bf16[8,128,2048]{2,1,0:T(8,128)(2,1)} %bitcast.2, s32[4,128]{1,0:T(4,128)} %tile_tables.1.table_ref.table_hbm, s32[4,128]{1,0:T(4,128)} %tile_tables.1.table_ref.table_hbm), custom_call_target="tpu_custom_call" | custom-call | flops 8589934592 | bytes 8388608 | tf_op jit(solution)/shard_map/exchange_and_multiply/pallas_call | solution.py:279
  213.8 3.2 %copy.6 = bf16[512,2048]{1,0:T(8,128)(2,1)} copy(bf16[512,2048]{1,0:T(8,128)(2,1)} %exchange_and_multiply.1) | data formatting | bytes 4194304

commit v2 on v1

v2 whole, which is shorter than its diff:
```python
import functools

import jax
import jax.numpy as jnp
from jax import lax
from jax.experimental import pallas as pl
from jax.experimental.pallas import tpu as pltpu
from jax.sharding import PartitionSpec as P

TILE = 128
RT, KT, CT = 4, 8, 16
CAP, CAPB = 24, 96
CHUNKS = 8
PER = CAPB // CHUNKS
WIDE = 256
PIECES = CT * TILE // WIDE
GROUPS = 8
SPAN = RT * TILE // GROUPS
TOP = 32767.0
MESH = pl.DeviceIdType.MESH
WITH_OWN, WITH_NEXT, LOCAL, NEXT, FAR = range(5)
TAKERS = (
    (WITH_OWN, 1, -1, 0), (WITH_OWN, 3, -3, 1),
    (WITH_NEXT, 1, -2, 0), (WITH_NEXT, 3, -2, 1),
    (LOCAL, 0, -1, 0), (LOCAL, 0, -3, 1),
)


def main_kernel(
    a_ref, b_ref, left_ref, right_ref, out_ref,
    a_slot, b_slot, a_after, b_after, a_table, b_table,
    a_in, b_in, a_pack, b_pack, a_got, a_near, b_got, b_stage, table_got, table_at,
    a_full, b_full, total, part, code_out, scale_out, code_in, scale_in, result,
    local_sem, table_send, table_recv, a_send, a_recv, b_send, b_recv, p_send, p_recv, out_sem,
):
    n_row, n_col = lax.axis_size("row"), lax.axis_size("col")
    row, col = lax.axis_index("row"), lax.axis_index("col")

    def at(i, j):
        return (lax.rem(row + i + n_row, n_row), lax.rem(col + j + n_col, n_col))

    def parity(i, j):
        return lax.rem(i + j, 2)

    odd = parity(row, col)
    takes = [jnp.where(parity(*at(i, j)) == want, 1, 0) for _, i, j, want in TAKERS]
    b_target, b_source = at(1 - 2 * odd, 0), at(1 - 2 * odd, 0)
    p_target, p_source = at(-1 - 2 * odd, 0), at(3 - 2 * odd, 0)
    far_target, far_source = at(-4, 0), at(4, 0)
    a_sources = (at(-1 - 2 * odd, 1 + 2 * odd), at(-1 - 2 * odd, 2), at(0, 1 + 2 * odd))

    barrier = pltpu.get_barrier_semaphore()
    for source in (*a_sources, b_source, p_source):
        pl.semaphore_signal(barrier, inc=1, device_id=source, device_id_type=MESH)

    @pl.when(odd == 1)
    def _():
        pl.semaphore_signal(barrier, inc=1, device_id=far_source, device_id_type=MESH)

    def load_a(k):
        return pltpu.make_async_copy(
            a_ref.at[:, :, pl.ds(k * TILE, TILE)], a_in.at[pl.ds(k * RT, RT)], local_sem.at[k])

    def load_b(c):
        return pltpu.make_async_copy(
            b_ref.at[:, :, pl.ds(c * TILE, TILE)], b_in.at[pl.ds(c * KT, KT)], local_sem.at[KT + c])

    for k in range(KT):
        load_a(k).start()
    for c in range(CT):
        load_b(c).start()

    blank = jnp.zeros((TILE, TILE), jnp.bfloat16)
    a_pack[CAP] = blank
    b_pack[CAPB] = blank
    for i in range(2):
        a_got[i, CAP] = blank
    a_near[CAP] = blank
    b_got[1, CAPB] = blank
    b_stage[CAPB] = blank

    def number(there, count, slot, after, blank_slot):
        def walk(t, taken):
            slot[0, t] = jnp.where(there(t) > 0, taken, blank_slot)
            return taken + jnp.where(there(t) > 0, 1, 0)

        lax.fori_loop(0, count, walk, 0)

        def back(n, found):
            t = count - 1 - n
            found = jnp.where(there(t) > 0, t, found)
            after[0, t] = found
            return found

        after[0, count] = count - 1
        lax.fori_loop(0, count, back, count - 1)

    def pack_a(n, start):
        t = a_after[0, start]
        a_pack[n] = a_in[t]
        return t + 1

    def pack_b(n, start):
        t = b_after[0, start]
        b_pack[n] = b_in[t]
        return t + 1

    def stage_b(n, carry):
        b_stage[n] = b_got[0, n]
        return carry

    def send_table(n, i, source, target):
        return pltpu.make_async_remote_copy(
            source, table_got.at[i], table_send.at[n], table_recv.at[i], device_id=target, device_id_type=MESH)

    def send_a(n):
        use, i, j, _ = TAKERS[n]
        place = a_near if use == LOCAL else a_got.at[use]
        return pltpu.make_async_remote_copy(
            a_pack.at[pl.ds(0, CAP)], place.at[pl.ds(0, CAP)], a_send.at[n], a_recv.at[use],
            device_id=at(i, j), device_id_type=MESH)

    def each_taker(uses, act):
        for n, (use, i, j, _) in enumerate(TAKERS):
            if use in uses:

                @pl.when(takes[n] == 1)
                def _():
                    act(send_table(n, use, a_table, at(i, j)))
                    act(send_a(n))

    def send_b(q):
        where = pl.ds(q * PER, PER)
        return pltpu.make_async_remote_copy(
            b_pack.at[where], b_got.at[0, where], b_send.at[0, q], b_recv.at[0, q],
            device_id=b_target, device_id_type=MESH)

    def send_far(q):
        where = pl.ds(q * PER, PER)
        return pltpu.make_async_remote_copy(
            b_got.at[0, where], b_got.at[1, where], b_send.at[1, q], b_recv.at[1, q],
            device_id=far_target, device_id_type=MESH)

    next_table = send_table(len(TAKERS), NEXT, b_table, b_target)
    far_table = send_table(len(TAKERS) + 1, FAR, table_got.at[NEXT], far_target)

    def send_code(c):
        return pltpu.make_async_remote_copy(
            code_out.at[c], code_in.at[c], p_send.at[0, c], p_recv.at[0, c], device_id=p_target, device_id_type=MESH)

    def send_scale(c):
        return pltpu.make_async_remote_copy(
            scale_out.at[c], scale_in.at[c], p_send.at[1, c], p_recv.at[1, c], device_id=p_target, device_id_type=MESH)

    def publish(slot, table):
        copy = pltpu.make_async_copy(slot, table, local_sem.at[KT + CT])
        copy.start()
        copy.wait()

    number(lambda t: left_ref[t % RT, t // RT], RT * KT, a_slot, a_after, CAP)
    publish(a_slot, a_table)
    for k in range(KT):
        load_a(k).wait()
    lax.fori_loop(0, CAP, pack_a, 0)
    pl.semaphore_wait(barrier, 2 + odd + sum(takes))
    each_taker((WITH_OWN, WITH_NEXT), lambda copy: copy.start())
    number(lambda t: right_ref[t % KT, t // KT], KT * CT, b_slot, b_after, CAPB)
    publish(b_slot, b_table)
    next_table.start()
    for c in range(CT):
        load_b(c).wait()
    lax.fori_loop(0, CAPB, pack_b, 0)
    send_b(0).start()
    send_b(1).start()

    def unpack_a(i, tile_of):
        for k in range(KT):
            for r in range(RT):
                a_full[i, r * TILE : (r + 1) * TILE, k * TILE : (k + 1) * TILE] = tile_of(k * RT + r)

    def unpack_b(i, tile_of, first, last):
        def one(c, carry):
            for half in range(WIDE // TILE):
                for k in range(KT):
                    tile = tile_of((c * (WIDE // TILE) + half) * KT + k)
                    b_full[i, c, k * TILE : (k + 1) * TILE, half * TILE : (half + 1) * TILE] = tile
            return carry

        lax.fori_loop(first, last, one, 0)

    def product(i, j, c):
        return jnp.dot(a_full[i], b_full[j, c], preferred_element_type=jnp.float32)

    unpack_a(3, lambda t: a_pack[a_slot[0, t]])
    unpack_b(0, lambda t: b_pack[b_slot[0, t]], 0, PIECES)

    def first_term(c, carry):
        total[c] = product(3, 0, c)
        return carry

    lax.fori_loop(0, PIECES, first_term, 0)

    def fetch_table(i):
        send_table(0, i, a_table, b_target).wait_recv()
        fetch = pltpu.make_async_copy(table_got.at[i], table_at.at[i], local_sem.at[KT + CT])
        fetch.start()
        fetch.wait()

    fetch_table(NEXT)

    @pl.when(odd == 1)
    def _():
        far_table.start()

    def part_own(c, carry):
        part[c] = product(WITH_OWN, 0, c)
        return carry

    early = CHUNKS - PIECES // 2
    for q in range(CHUNKS):
        if q + 2 < CHUNKS:
            send_b(q).wait_send()
            send_b(q + 2).start()
        if q == early:
            for i in (WITH_OWN, WITH_NEXT):
                fetch_table(i)
                send_a(2 * i).wait_recv()
            for i in (WITH_OWN, WITH_NEXT):
                unpack_a(i, lambda t: a_got[i, table_at[i, 0, t]])
        if q >= early:
            lax.fori_loop(2 * (q - early), 2 * (q - early) + 2, part_own, 0)
        send_b(q).wait_recv()

        @pl.when(odd == 1)
        def _():
            send_far(q).start()

        lax.fori_loop(q * PER, (q + 1) * PER, stage_b, 0)

    for c in range(PIECES):
        unpack_b(1, lambda t: b_stage[table_at[NEXT, 0, t]], c, c + 1)
        part[c] += product(WITH_NEXT, 1, c)
        for g in range(GROUPS):
            rows = slice(g * SPAN, (g + 1) * SPAN)
            values = part[c, rows, :]
            most = jnp.maximum(jnp.max(jnp.abs(values), axis=0, keepdims=True), 1e-33)
            code_out[c, rows, :] = jnp.round(values * (TOP / most)).astype(jnp.int32).astype(jnp.int16)
            scale_out[c, g : g + 1, :] = most * (1.0 / TOP)
        if c >= 3:
            send_code(c - 3).wait_send()
        send_scale(c).start()
        send_code(c).start()
        if c == 1:
            each_taker((LOCAL,), lambda copy: copy.start())

    @pl.when(odd == 1)
    def _():
        fetch_table(FAR)
        for q in range(CHUNKS):
            send_far(q).wait_recv()
        unpack_b(1, lambda t: b_got[1, table_at[FAR, 0, t]], 0, PIECES)

    fetch_table(LOCAL)
    send_a(2 * LOCAL).wait_recv()
    unpack_a(LOCAL, lambda t: a_near[table_at[LOCAL, 0, t]])

    def second_term(c, carry):
        total[c] += product(LOCAL, 1, c)
        return carry

    lax.fori_loop(0, PIECES, second_term, 0)

    def store(c):
        return pltpu.make_async_copy(result.at[c], out_ref.at[:, pl.ds(c * WIDE, WIDE)], out_sem.at[c])

    for c in range(PIECES):
        send_scale(c).wait_recv()
        send_code(c).wait_recv()
        for g in range(GROUPS):
            rows = slice(g * SPAN, (g + 1) * SPAN)
            other = code_in[c, rows, :].astype(jnp.int32).astype(jnp.float32) * scale_in[c, g : g + 1, :]
            result[c, rows, :] = (total[c, rows, :] + other).astype(jnp.bfloat16)
        store(c).start()

    each_taker((WITH_OWN, WITH_NEXT, LOCAL), lambda copy: copy.wait_send())
    next_table.wait_send()
    for q in range(CHUNKS - 2, CHUNKS):
        send_b(q).wait_send()

    @pl.when(odd == 1)
    def _():
        far_table.wait_send()
        for q in range(CHUNKS):
            send_far(q).wait_send()

    for c in range(PIECES):
        send_scale(c).wait_send()
        if c >= PIECES - 3:
            send_code(c).wait_send()
        store(c).wait()


def per_device(left_panels, right_panels, left_pattern, right_pattern):
    smem = pl.BlockSpec(memory_space=pltpu.SMEM)
    anywhere = pl.BlockSpec(memory_space=pl.ANY)
    rows, cols, inner = RT * TILE, CT * TILE, KT * TILE
    bf16, f32, dma = jnp.bfloat16, jnp.float32, pltpu.SemaphoreType.DMA
    return pl.pallas_call(
        main_kernel,
        out_shape=jax.ShapeDtypeStruct((rows, cols), bf16),
        in_specs=[anywhere, anywhere, smem, smem],
        out_specs=anywhere,
        scratch_shapes=[
            pltpu.SMEM((1, TILE), jnp.int32),
            pltpu.SMEM((1, TILE), jnp.int32),
            pltpu.SMEM((1, 2 * TILE), jnp.int32),
            pltpu.SMEM((1, 2 * TILE), jnp.int32),
            pltpu.VMEM((1, TILE), jnp.int32),
            pltpu.VMEM((1, TILE), jnp.int32),
            pltpu.VMEM((RT * KT, TILE, TILE), bf16),
            pltpu.VMEM((KT * CT, TILE, TILE), bf16),
            pltpu.VMEM((CAP + 1, TILE, TILE), bf16),
            pltpu.VMEM((CAPB + 1, TILE, TILE), bf16),
            pltpu.VMEM((2, CAP + 1, TILE, TILE), bf16),
            pltpu.VMEM((CAP + 1, TILE, TILE), bf16),
            pltpu.VMEM((2, CAPB + 1, TILE, TILE), bf16),
            pltpu.VMEM((CAPB + 1, TILE, TILE), bf16),
            pltpu.VMEM((5, 1, TILE), jnp.int32),
            pltpu.SMEM((5, 1, TILE), jnp.int32),
            pltpu.VMEM((4, rows, inner), bf16),
            pltpu.VMEM((2, PIECES, inner, WIDE), bf16),
            pltpu.VMEM((PIECES, rows, WIDE), f32),
            pltpu.VMEM((PIECES, rows, WIDE), f32),
            pltpu.VMEM((PIECES, rows, WIDE), jnp.int16),
            pltpu.VMEM((PIECES, GROUPS, WIDE), f32),
            pltpu.VMEM((PIECES, rows, WIDE), jnp.int16),
            pltpu.VMEM((PIECES, GROUPS, WIDE), f32),
            pltpu.VMEM((PIECES, rows, WIDE), bf16),
            dma((KT + CT + 1,)),
            dma((len(TAKERS) + 2,)),
            dma((5,)),
            dma((len(TAKERS),)),
            dma((3,)),
            dma((2, CHUNKS)),
            dma((2, CHUNKS)),
            dma((2, PIECES)),
            dma((2, PIECES)),
            dma((PIECES,)),
        ],
        compiler_params=pltpu.CompilerParams(
            collective_id=0, has_side_effects=True, vmem_limit_bytes=60 * 2**20
        ),
        cost_estimate=pl.CostEstimate(flops=8 * rows * inner * cols, bytes_accessed=2**23, transcendentals=0),
        name="exchange_and_multiply",
    )(left_panels.reshape(RT, TILE, inner), right_panels.reshape(KT, TILE, cols), left_pattern, right_pattern)


def solution(mesh):
    placed = (P("row", "col"), P("row", "col"), P("row", "col"), P("row", "col"))
    return jax.shard_map(
        per_device, mesh=mesh, in_specs=placed, out_specs=P("row", "col"), check_vma=False
    )
```

time: 217 us -> 201 us (0.926)
  the two profiles are of different devices: /device:TPU:201 before, /device:TPU:194 now
where the time goes in v2:
time: 201 us
  Pallas kernels  197 us (98%)
  local copies, waits for them, and re-layouts  3.16 us (2%)
    pallas_call x1, Pallas kernels, per_device(): pl.pallas_call(main_kernel, out_shape=jax.ShapeDtypeStruct((rows, cols),...  197 us

profile of v2, /device:TPU:194, one launch (start us, length us, event | category | flops | bytes accessed | tf_op | source)
XLA Modules:
  0.0 200.7 jit_solution(9449429446732401736)
XLA Ops:
  0.0 197.5 %exchange_and_multiply.1 = bf16[512,2048]{1,0:T(8,128)(2,1)} custom-call(bf16[4,128,1024]{2,1,0:T(8,128)(2,1)} %bitcast.3, bf16[8,128,2048]{2,1,0:T(8,128)(2,1)} %bitcast.2, s32[4,8]{1,0:T(4,128)} %left_ref.1, s32[8,16]{1,0:T(8,128)} %right_ref.1), custom_call_target="tpu_custom_call" | custom-call | flops 8589934592 | bytes 8388608 | tf_op jit(solution)/shard_map/exchange_and_multiply/pallas_call | solution.py:308
  197.5 3.2 %copy.6 = bf16[512,2048]{1,0:T(8,128)(2,1)} copy(bf16[512,2048]{1,0:T(8,128)(2,1)} %exchange_and_multiply.1) | data formatting | bytes 4194304

commit v3 on v2

--- a/solution.py
+++ b/solution.py
@@ -171,7 +171,6 @@
         load_b(c).wait()
     lax.fori_loop(0, CAPB, pack_b, 0)
     send_b(0).start()
-    send_b(1).start()
 
     def unpack_a(i, tile_of):
         for k in range(KT):
@@ -218,9 +217,9 @@
 
     early = CHUNKS - PIECES // 2
     for q in range(CHUNKS):
-        if q + 2 < CHUNKS:
+        if q + 1 < CHUNKS:
             send_b(q).wait_send()
-            send_b(q + 2).start()
+            send_b(q + 1).start()
         if q == early:
             for i in (WITH_OWN, WITH_NEXT):
                 fetch_table(i)
@@ -284,7 +283,7 @@
 
     each_taker((WITH_OWN, WITH_NEXT, LOCAL), lambda copy: copy.wait_send())
     next_table.wait_send()
-    for q in range(CHUNKS - 2, CHUNKS):
+    for q in range(CHUNKS - 1, CHUNKS):
         send_b(q).wait_send()
 
     @pl.when(odd == 1)

time: 201 us -> 187 us (0.930)
  the two profiles are of different devices: /device:TPU:194 before, /device:TPU:2 now
where the time goes in v3:
time: 187 us; the launch traced here: 186 us
  Pallas kernels  183 us (98%)
  local copies, waits for them, and re-layouts  3.16 us (2%)
    pallas_call x1, Pallas kernels, per_device(): pl.pallas_call(main_kernel, out_shape=jax.ShapeDtypeStruct((rows, cols),...  183 us

profile of v3, /device:TPU:2, one launch (start us, length us, event | category | flops | bytes accessed | tf_op | source)
XLA Modules:
  0.0 186.1 jit_solution(17518857231788523483)
XLA Ops:
  0.0 182.9 %exchange_and_multiply.1 = bf16[512,2048]{1,0:T(8,128)(2,1)} custom-call(bf16[4,128,1024]{2,1,0:T(8,128)(2,1)} %bitcast.3, bf16[8,128,2048]{2,1,0:T(8,128)(2,1)} %bitcast.2, s32[4,8]{1,0:T(4,128)} %left_ref.1, s32[8,16]{1,0:T(8,128)} %right_ref.1), custom_call_target="tpu_custom_call" | custom-call | flops 8589934592 | bytes 8388608 | tf_op jit(solution)/shard_map/exchange_and_multiply/pallas_call | solution.py:307
  182.9 3.2 %copy.6 = bf16[512,2048]{1,0:T(8,128)(2,1)} copy(bf16[512,2048]{1,0:T(8,128)(2,1)} %exchange_and_multiply.1) | data formatting | bytes 4194304

commit v4 on v3

--- a/solution.py
+++ b/solution.py
@@ -220,6 +220,8 @@
         if q + 1 < CHUNKS:
             send_b(q).wait_send()
             send_b(q + 1).start()
+        if q + 1 == CHUNKS:
+            each_taker((LOCAL,), lambda copy: copy.start())
         if q == early:
             for i in (WITH_OWN, WITH_NEXT):
                 fetch_table(i)
@@ -249,8 +251,6 @@
             send_code(c - 3).wait_send()
         send_scale(c).start()
         send_code(c).start()
-        if c == 1:
-            each_taker((LOCAL,), lambda copy: copy.start())
 
     @pl.when(odd == 1)
     def _():

time: 187 us -> 184 us (0.984)
  Pallas kernels: 183 us -> 180 us
    pallas_call x1, Pallas kernels: 183 us -> 180 us  [per_device(): pl.pallas_call(main_kernel, out_shape=jax.ShapeDtypeStruct((rows, cols),...]
where the time goes in v4:
time: 184 us
  Pallas kernels  180 us (98%)
  local copies, waits for them, and re-layouts  3.16 us (2%)
    pallas_call x1, Pallas kernels, per_device(): pl.pallas_call(main_kernel, out_shape=jax.ShapeDtypeStruct((rows, cols),...  180 us

profile of v4, /device:TPU:2, one launch (start us, length us, event | category | flops | bytes accessed | tf_op | source)
XLA Modules:
  0.0 183.5 jit_solution(7393131188336602286)
XLA Ops:
  0.0 180.3 %exchange_and_multiply.1 = bf16[512,2048]{1,0:T(8,128)(2,1)} custom-call(bf16[4,128,1024]{2,1,0:T(8,128)(2,1)} %bitcast.3, bf16[8,128,2048]{2,1,0:T(8,128)(2,1)} %bitcast.2, s32[4,8]{1,0:T(4,128)} %left_ref.1, s32[8,16]{1,0:T(8,128)} %right_ref.1), custom_call_target="tpu_custom_call" | custom-call | flops 8589934592 | bytes 8388608 | tf_op jit(solution)/shard_map/exchange_and_multiply/pallas_call | solution.py:307
  180.3 3.2 %copy.6 = bf16[512,2048]{1,0:T(8,128)(2,1)} copy(bf16[512,2048]{1,0:T(8,128)(2,1)} %exchange_and_multiply.1) | data formatting | bytes 4194304

commit v5 on v4

--- a/solution.py
+++ b/solution.py
@@ -220,7 +220,7 @@
         if q + 1 < CHUNKS:
             send_b(q).wait_send()
             send_b(q + 1).start()
-        if q + 1 == CHUNKS:
+        if q + 2 == CHUNKS:
             each_taker((LOCAL,), lambda copy: copy.start())
         if q == early:
             for i in (WITH_OWN, WITH_NEXT):

time: 184 us -> 184 us (level)
  no operation moved by 1% of the time
where the time goes in v5:
time: 184 us; the launch traced here: 183 us
  Pallas kernels  180 us (98%)
  local copies, waits for them, and re-layouts  3.16 us (2%)
    pallas_call x1, Pallas kernels, per_device(): pl.pallas_call(main_kernel, out_shape=jax.ShapeDtypeStruct((rows, cols),...  180 us

profile of v5, /device:TPU:2, one launch (start us, length us, event | category | flops | bytes accessed | tf_op | source)
XLA Modules:
  0.0 183.5 jit_solution(9097835079848940193)
XLA Ops:
  0.0 180.3 %exchange_and_multiply.1 = bf16[512,2048]{1,0:T(8,128)(2,1)} custom-call(bf16[4,128,1024]{2,1,0:T(8,128)(2,1)} %bitcast.3, bf16[8,128,2048]{2,1,0:T(8,128)(2,1)} %bitcast.2, s32[4,8]{1,0:T(4,128)} %left_ref.1, s32[8,16]{1,0:T(8,128)} %right_ref.1), custom_call_target="tpu_custom_call" | custom-call | flops 8589934592 | bytes 8388608 | tf_op jit(solution)/shard_map/exchange_and_multiply/pallas_call | solution.py:307
  180.3 3.2 %copy.6 = bf16[512,2048]{1,0:T(8,128)(2,1)} copy(bf16[512,2048]{1,0:T(8,128)(2,1)} %exchange_and_multiply.1) | data formatting | bytes 4194304
